TPU v7x, 256 devices: a whole 4x4x8 slice. The times are simulated.
256 devices in a mesh: grp: 8 (over z_hi, y), seg: 32 (over z_lo, x, core).
Axes of the slice: x: 4, y: 4, z: 8 (z_hi: 2, z_lo: 4; z = z_hi * 4 + z_lo), core: 2. Of those that a mesh axis runs over, the one named last changes fastest.
Arguments:
- waveform: bfloat16 [2048, 512, 512], P('grp', 'seg')
- valid_count: int32 [2048, 512], P('grp', 'seg'), may hold values from 128 to 512
- plan: int32 [8, 8], replicated, may hold values from 0 to 7, as said below
Outputs:
- cross: bfloat16 [128, 2, 2048, 8, 256], P('seg', None, 'grp')
Inputs may be any that keep to these rules, and one draw needn't show every extreme that they name: `plan`: row g lists, round by round, the partner group of group g: in every round g is the partner of its partner and each group is named once, and every row names each of the 8 groups at least once.
All inputs are finite; a program needn't handle non-finite values.
Results may differ from a plain program's by a relative error of at most 0.0061.
Values may be sent and summed in bfloat16 or wider, within the bound.
A program may use at most 128 MiB of HBM per device.

v0:
```python
import math

import jax
import jax.numpy as jnp
from jax import lax
from jax.sharding import PartitionSpec as P

F = 128
K0 = 2


def make_basis(samples):
    times = jnp.arange(samples, dtype=jnp.int32)[:, None]
    bins = K0 + jnp.arange(F, dtype=jnp.int32)[None, :]
    phase = (times * bins % samples).astype(jnp.float32) * (2.0 * math.pi / samples)
    return jnp.concatenate([jnp.cos(phase), -jnp.sin(phase)], axis=1).astype(jnp.bfloat16)


def add_block(carry, piece, start, left_side, group_rows):
    count = piece.shape[3]
    span = min(count, group_rows)
    seg_total = left_side.shape[2] // 2
    for portion in range(count // span):
        partner = piece[:, :, :, portion * span : (portion + 1) * span]
        right_side = jnp.concatenate([partner[0], partner[1]], axis=1)
        block = jnp.einsum(
            "cbsi,bsj->bcij", left_side, right_side, preferred_element_type=jnp.float32
        )
        block = (block / float(seg_total)).astype(jnp.bfloat16)
        first = start + portion * span
        owner = jnp.asarray(first // group_rows, dtype=jnp.int32)
        offset = jnp.asarray(first % group_rows, dtype=jnp.int32)
        zero = jnp.asarray(0, dtype=jnp.int32)
        carry = lax.dynamic_update_slice(
            carry, block[:, :, :, None, :], (zero, zero, zero, owner, offset)
        )
    return carry


def shards(waveform, valid_count, plan):
    group_rows, seg_local, samples = waveform.shape
    basis = make_basis(samples)
    times = lax.broadcasted_iota(jnp.int32, waveform.shape, 2)
    gated = jnp.where(times < valid_count[:, :, None], waveform, jnp.zeros_like(waveform))
    spectrum = jnp.einsum("tk,ist->ksi", basis, gated, preferred_element_type=jnp.float32)
    spectrum = spectrum.reshape(2, F, seg_local, group_rows)
    power = jnp.sum(spectrum * spectrum, axis=(0, 1)) / F
    keep = (valid_count.T >= samples // 2).astype(jnp.float32)
    weight = keep / jnp.sqrt(power + 1e-06)
    white = (spectrum * weight[None, None, :, :]).astype(jnp.bfloat16)
    group_index = lax.axis_index("grp")
    sched_row = lax.dynamic_index_in_dim(plan, group_index, 0, keepdims=False)
    mine = lax.all_to_all(white, "seg", split_axis=1, concat_axis=2, tiled=True)
    real_part = mine[0]
    imag_part = mine[1]
    left_side = jnp.stack(
        [
            jnp.concatenate([real_part, imag_part], axis=1),
            jnp.concatenate([imag_part, -real_part], axis=1),
        ],
        axis=0,
    )
    bins_local = mine.shape[1]
    groups_total = lax.axis_size("grp")
    empty = jnp.zeros((bins_local, 2, group_rows, groups_total, group_rows), jnp.bfloat16)
    everyone_bins = lax.all_gather(mine, "grp", axis=3, tiled=True)
    per_group = add_block(empty, everyone_bins, 0, left_side, group_rows)
    return jnp.take(per_group, sched_row, axis=3)


def solution(mesh):
    return jax.shard_map(
        shards,
        mesh=mesh,
        in_specs=(P("grp", "seg", None), P("grp", "seg"), P()),
        out_specs=P("seg", None, "grp", None, None),
        check_vma=False,
    )
```

profile of v0, /device:TPU:2, one launch (start us, length us, event | category | flops | bytes accessed | tf_op | source)
XLA Modules:
  0.0 466.3 jit_solution(499309325123212689)
XLA Ops:
  6.5 1.2 cosine_convert_fusion
  7.8 0.8 copy.29
  8.6 2.9 fusion
  11.5 3.0 fusion.1
  14.5 2.3 fusion.2
  16.8 57.3 %all_to_all.18 = bf16[2,128,16,256]{3,2,0,1:T(8,128)(2,1)S(1)} all-to-all(bf16[2,128,16,256]{3,2,0,1:T(8,128)(2,1)S(1)} %fusion.2), channel_id=1, replica_groups=mesh['grp'=8,'seg'=32] {'seg'}, dimensions={1} | all-to-all | bytes 4194304 | tf_op jit(solution)/shard_map/all_to_all | solution.py:53
  74.1 1.5 copy.39
  77.2 1.2 fusion.62
  79.0 1.3 copy.33
  81.1 2.5 maximum_bitcast_fusion
  83.6 317.6 %all-gather.2.cloned.1.call-done = bf16[2,4,512,2048]{3,2,1,0:T(8,128)(2,1)} async-done(((bf16[2,4,512,256]{3,2,1,0:T(8,128)(2,1)}), bf16[2,4,512,2048]{3,2,1,0:T(8,128)(2,1)}) %all-gather.2.cloned.1.call-update) | async-done | bytes 16777232 | tf_op jit(solution)/shard_map/all_gather | solution.py:66
  401.2 7.1 %slice_bitcast_fusion.1 = (bf16[4,512,256]{2,1,0:T(8,128)(2,1)S(1)}, bf16[4,512,256]{2,1,0:T(8,128)(2,1)S(1)}, bf16[4,512,256]{2,1,0:T(8,128)(2,1)S(1)}, bf16[4,...) fusion(bf16[2,4,512,2048]{3,2,1,0:T(8,128)(2,1)} %all-gather.2., ...), kind=kLoop, calls=%fused_computation.69 | loop fusion | bytes 33554432 | tf_op jit(solution)/shard_map/squeeze | solution.py:25
  408.4 2.3 fusion.29
  410.6 5.6 %dynamic_update_slice.24 = bf16[4,2,256,8,256]{4,2,1,0,3:T(8,128)(2,1)} pad(bf16[4,2,256,1,256]{4,2,1,0,3:T(8,128)(2,1)} %fusion.29, bf16[]{:T(256)} %constant.64.clone.1), padding=0_0x0_0x0_0x0_7x0_0 | pad | bytes 9437186 | tf_op jit(solution)/shard_map/dynamic_update_slice | solution.py:34
  416.2 2.2 fusion.31
  418.4 2.2 fusion.33
  420.7 2.2 fusion.35
  422.9 2.2 fusion.37
  425.2 2.2 fusion.39
  427.4 2.2 fusion.41
  429.7 2.2 fusion.43
  431.9 8.1 %gather_fusion = bf16[8,4,2,256,256]{4,3,2,1,0:T(8,128)(2,1)} fusion(bf16[4,2,256,8,256]{4,2,1,0,3:T(8,128)(2,1)} %fusion.43, s32[1024]{0:T(1024)S(1)} %pad_clamp_fusion), kind=kCustom, calls=%fused_computation | custom fusion | bytes 16777248 | tf_op jit(solution)/shard_map/jit(_take)/gather | solution.py:68
  440.0 7.5 %select_bitcast_fusion = bf16[4,2,256,8,256]{4,2,1,0,3:T(8,128)(2,1)} fusion(bf16[8,4,2,256,256]{4,3,2,1,0:T(8,128)(2,1)} %gather_fusion, pred[8]{0:T(512)(128)(4,1)S(1)} %compare_and_fusion), kind=kLoop, calls=%fused_computation.1 | loop fusion | flops 4194304 | bytes 16777224 | tf_op jit(solution)/shard_map/jit(_take)/select_n | solution.py:68
  447.5 11.9 %copy.40 = bf16[4,2,256,8,256]{4,3,2,1,0:T(8,128)(2,1)} copy(bf16[4,2,256,8,256]{4,2,1,0,3:T(8,128)(2,1)} %select_bitcast_fusion) | data formatting | bytes 16777216 | tf_op jit(solution)/shard_map/jit(_take)/select_n | solution.py:68
  (18 shorter events, 3.0 us)
Async XLA Ops:
  6.5 394.7 %all-gather.2.cloned.1.call-start = ((), (), s32[]{:S(2)}) async-start(), calls=%async_computation.1 | async-start | bytes 18874368 | tf_op jit(solution)/shard_map/all_gather | solution.py:66
  11.5 3.0 copy-start.2
  83.6 324.7 %copy-start = (bf16[1,4,1024,256]{2,3,0,1:T(8,128)(2,1)S(1)}, bf16[1,4,1024,256]{2,3,0,1:T(8,128)(2,1)}, u32[]{:S(2)}) copy-start(bf16[1,4,1024,256]{2,3,0,1:T(8,128)(2,1)} %get-tuple-element.23) | copy-start | bytes 6291460
  401.2 7.1 %copy-start.1 = (bf16[1,4,1024,256]{2,3,0,1:T(8,128)(2,1)S(1)}, bf16[1,4,1024,256]{2,3,0,1:T(8,128)(2,1)}, u32[]{:S(2)}) copy-start(bf16[1,4,1024,256]{2,3,0,1:T(8,128)(2,1)} %get-tuple-element.24) | copy-start | bytes 6291460
Sparse Core Ops, SparseCore 0:
  75.8 325.4 all-gather.1
where the time goes:
time: 467 us; the launch traced here: 466 us
  waiting for transfers between devices  318 us (68%)
  blocking collectives  57.3 us (12%)
  local copies, waits for them, and re-layouts  38.8 us (8%)
  matrix products  21 us (4%)
  other arithmetic  18 us (4%)
  between operations  13.5 us (3%)
    all_gather x1, waiting for transfers between devices, shards(): everyone_bins = lax.all_gather(mine, 'grp', axis=3, tiled=True)  318 us
    all_to_all x1, blocking collectives, shards(): mine = lax.all_to_all(white, 'seg', split_axis=1, concat_axis=2, tiled=True)  57.3 us
    dot_general x8, matrix products, add_block(): jnp.einsum('cbsi,bsj->bcij', left_side, right_side, preferred_element_typ...  18 us
    select_n x1, local copies, waits for them, and re-layouts, shards(): return jnp.take(per_group, sched_row, axis=3)  11.9 us
  transfers between devices with their start and end apart: 1, of which 1 were waited for; matrix products, arithmetic and copies ran while one was open for 2% of the time, Pallas kernels for 0%

commit v1 on v0

v1 whole, which is shorter than its diff:
```python
import functools
import math

import jax
import jax.numpy as jnp
from jax import lax
from jax.experimental import pallas as pl
from jax.experimental.pallas import tpu as pltpu
from jax.sharding import PartitionSpec as P

F = 128
K0 = 2
MESH = pl.DeviceIdType.MESH

NY = 4
NZ = 2
NS = 32
PEERS = NZ * NS
BINS = 4
ROWS = 32
DEPTH = NS * ROWS
G = 256
NGRP = NZ * NY
TILE = 16


def make_basis(samples):
    times = jnp.arange(samples, dtype=jnp.int32)[:, None]
    bins = K0 + jnp.arange(F, dtype=jnp.int32)[None, :]
    phase = (times * bins % samples).astype(jnp.float32) * (2.0 * math.pi / samples)
    return jnp.concatenate([jnp.cos(phase), -jnp.sin(phase)], axis=1).astype(jnp.bfloat16)


def transpose_left(source, index, left):
    def step(c, carry):
        block = source[index, pl.ds(pl.multiple_of(c * 128, 128), 128), :]
        parts = block.reshape(8, 16, G)
        turned = []
        for m in range(4):
            turned += [parts[2 * m + 1], -parts[2 * m]]
        other = jnp.concatenate(turned, axis=0)
        at = pl.ds(pl.multiple_of(c * 128, 128), 128)
        left[pl.ds(0, G), at] = block.T
        left[pl.ds(G, G), at] = other.T
        return carry

    lax.fori_loop(0, DEPTH // 128, step, 0)


def product(left, right):
    full = jnp.dot(left[...], right, preferred_element_type=jnp.float32)
    return (full * (1.0 / 512.0)).astype(jnp.bfloat16)


def kernel(plan_ref, white, out, *scratch):
    spec = scratch[0:4]
    res = scratch[4:8]
    done = scratch[8:12]
    give, left, tmp = scratch[12:15]
    send1, recv1, send2, recv2, send3, recv3, out_sem = scratch[15:]
    g = lax.axis_index("grp")
    s = lax.axis_index("seg")
    zh, y = lax.div(g, NY), lax.rem(g, NY)
    me = zh * NS + s
    right = zh * NY + lax.rem(y + 1, NY)
    leftd = zh * NY + lax.rem(y + NY - 1, NY)

    def peer(d):
        p = lax.rem(me + d, PEERS)
        return lax.div(p, NS), lax.rem(p, NS)

    barrier = pltpu.get_barrier_semaphore()

    def greet(d, carry):
        pz, ps = peer(d)
        pl.semaphore_signal(barrier, inc=1, device_id=(pz * NY + y, ps), device_id_type=MESH)
        return carry

    lax.fori_loop(1, PEERS, greet, 0)
    for n in (right, leftd):
        pl.semaphore_signal(barrier, inc=1, device_id=(n, s), device_id_type=MESH)
    pl.semaphore_wait(barrier, PEERS + 1)

    mine = pl.ds(pl.multiple_of(s * ROWS, ROWS), ROWS)

    def scatter(b):
        def send(d, carry):
            pz, ps = peer(d)
            pltpu.make_async_remote_copy(
                src_ref=white.at[ps * BINS + b],
                dst_ref=spec[b].at[2 + zh, mine],
                send_sem=send1.at[b],
                recv_sem=recv1.at[b],
                device_id=(pz * NY + y, ps),
                device_id_type=MESH,
            ).start()
            return carry

        lax.fori_loop(1, PEERS, send, 0)
        pltpu.make_async_copy(white.at[s * BINS + b], spec[b].at[2 + zh, mine], recv1.at[b]).start()

    def scatter_arrived(b):
        own = spec[b].at[pl.ds(2, 2)]
        pltpu.make_async_copy(own, own, recv1.at[b]).wait()

    def scatter_left(b):
        some = white.at[pl.ds(0, PEERS - 1)]
        pltpu.make_async_copy(some, some, send1.at[b]).wait()

    def neighbour(b, side):
        to, at = ((right, 0), (leftd, 4))[side]
        return pltpu.make_async_remote_copy(
            src_ref=spec[b].at[pl.ds(2, 2)],
            dst_ref=spec[b].at[pl.ds(at, 2)],
            send_sem=send2.at[b, side],
            recv_sem=recv2.at[b, side],
            device_id=(to, s),
            device_id_type=MESH,
        )

    def gift(b, side):
        to, group = ((right, lax.rem(y + 3, NY)), (leftd, NY + lax.rem(y + 1, NY)))[side]
        return pltpu.make_async_remote_copy(
            src_ref=give.at[b, side],
            dst_ref=res[b].at[group],
            send_sem=send3.at[b, side],
            recv_sem=recv3.at[b, side],
            device_id=(to, s),
            device_id_type=MESH,
        )

    def multiply(b):
        transpose_left(spec[b], 4 + zh, left)
        give[b, 0] = product(left, spec[b][0])
        gift(b, 0).start()
        transpose_left(spec[b], zh, left)
        give[b, 1] = product(left, spec[b][5])
        gift(b, 1).start()
        transpose_left(spec[b], 2 + zh, left)

        def block(t, carry):
            group = lax.rem(t, 2) * NY + lax.rem(y + 3 + lax.div(t, 2), NY)
            res[b][group] = product(left, spec[b][t])
            return carry

        lax.fori_loop(0, 6, block, 0)

    def assemble(b):
        def tile(m, carry):
            rows = pl.ds(pl.multiple_of(m * TILE, TILE), TILE)
            for r in range(NGRP):
                piece = res[b][plan_ref[g, r], rows, :].astype(jnp.float32)
                for h in range(2):
                    tmp[h, pl.ds(r, TILE, NGRP), :] = piece[:, h * 128 : h * 128 + 128]
            at = pl.ds(pl.multiple_of(m * TILE * NGRP, TILE * NGRP), TILE * NGRP)
            for h in range(2):
                done[b][at, h * 128 : h * 128 + 128] = tmp[h].astype(jnp.bfloat16)
            return carry

        lax.fori_loop(0, 2 * G // TILE, tile, 0)
        pltpu.make_async_copy(done[b], out.at[b], out_sem.at[b]).start()

    scatter(0)
    scatter(1)
    for b in range(BINS + 1):
        if b < BINS:
            scatter_arrived(b)
            for side in range(2):
                neighbour(b, side).start()
            if b + 2 < BINS:
                scatter(b + 2)
        if b >= 1:
            for side in range(2):
                neighbour(b - 1, side).wait_recv()
            multiply(b - 1)
            if b >= 2:
                for side in range(2):
                    gift(b - 2, side).wait_recv()
                assemble(b - 2)
    for side in range(2):
        gift(BINS - 1, side).wait_recv()
    assemble(BINS - 1)
    for b in range(BINS):
        scatter_left(b)
        for side in range(2):
            neighbour(b, side).wait_send()
            gift(b, side).wait_send()
        pltpu.make_async_copy(done[b], out.at[b], out_sem.at[b]).wait()


def cross(plan, white):
    bf16 = jnp.bfloat16
    return pl.pallas_call(
        kernel,
        out_shape=jax.ShapeDtypeStruct((BINS, 2 * G * NGRP, G), bf16),
        in_specs=[
            pl.BlockSpec(memory_space=pltpu.SMEM),
            pl.BlockSpec(memory_space=pltpu.VMEM),
        ],
        out_specs=pl.BlockSpec(memory_space=pl.ANY),
        scratch_shapes=[pltpu.VMEM((6, DEPTH, G), bf16)] * BINS
        + [pltpu.VMEM((NGRP, 2 * G, G), bf16)] * BINS
        + [pltpu.VMEM((2 * G * NGRP, G), bf16)] * BINS
        + [
            pltpu.VMEM((BINS, 2, 2 * G, G), bf16),
            pltpu.VMEM((2 * G, DEPTH), bf16),
            pltpu.VMEM((2, TILE * NGRP, 128), jnp.float32),
            pltpu.SemaphoreType.DMA((BINS,)),
            pltpu.SemaphoreType.DMA((BINS,)),
            pltpu.SemaphoreType.DMA((BINS, 2)),
            pltpu.SemaphoreType.DMA((BINS, 2)),
            pltpu.SemaphoreType.DMA((BINS, 2)),
            pltpu.SemaphoreType.DMA((BINS, 2)),
            pltpu.SemaphoreType.DMA((BINS,)),
        ],
        compiler_params=pltpu.CompilerParams(
            collective_id=0, has_side_effects=True, vmem_limit_bytes=56 * 1024 * 1024
        ),
    )(plan, white)


def shards(waveform, valid_count, plan):
    group_rows, seg_local, samples = waveform.shape
    basis = make_basis(samples)
    times = lax.broadcasted_iota(jnp.int32, waveform.shape, 2)
    gated = jnp.where(times < valid_count[:, :, None], waveform, jnp.zeros_like(waveform))
    spectrum = jnp.einsum("tk,ist->ksi", basis, gated, preferred_element_type=jnp.float32)
    spectrum = spectrum.reshape(2, F, seg_local, group_rows)
    power = jnp.sum(spectrum * spectrum, axis=(0, 1)) / F
    keep = (valid_count.T >= samples // 2).astype(jnp.float32)
    weight = keep / jnp.sqrt(power + 1e-06)
    white = (spectrum * weight[None, None, :, :]).astype(jnp.bfloat16)
    white = white.transpose(1, 0, 2, 3).reshape(F, ROWS, G)
    return cross(plan, white).reshape(BINS, 2, G, NGRP, G)


def solution(mesh):
    return jax.shard_map(
        shards,
        mesh=mesh,
        in_specs=(P("grp", "seg", None), P("grp", "seg"), P()),
        out_specs=P("seg", None, "grp", None, None),
        check_vma=False,
    )
```

time: 467 us -> 177 us (0.38)
  waiting for transfers between devices: 318 us -> 0 us
  Pallas kernels: 0 us -> 155 us
  blocking collectives: 57.3 us -> 0 us
  local copies, waits for them, and re-layouts: 38.8 us -> 8.14 us
  matrix products: 21 us -> 3.02 us
  between operations: 13.5 us -> 0.06 us
  other arithmetic: 18 us -> 7.75 us
    all_gather x1 -> x0, waiting for transfers between devices: 318 us -> none  [shards(): everyone_bins = lax.all_gather(mine, 'grp', axis=3, tiled=True)]
    pallas_call x0 -> x1, Pallas kernels: none -> 155 us  [cross(): pl.pallas_call(kernel, out_shape=jax.ShapeDtypeStruct((BINS, 2 * G * NGRP...]
    all_to_all x1 -> x0, blocking collectives: 57.3 us -> none  [shards(): mine = lax.all_to_all(white, 'seg', split_axis=1, concat_axis=2, tiled=True)]
    dot_general x8 -> x0, matrix products: 18 us -> none  [add_block(): jnp.einsum('cbsi,bsj->bcij', left_side, right_side, preferred_element_typ...]
    select_n x1 -> x0, local copies, waits for them, and re-layouts: 11.9 us -> none  [shards(): return jnp.take(per_group, sched_row, axis=3)]
    squeeze x3 -> x0, local copies, waits for them, and re-layouts: 8.19 us -> none  [the longest x1 7.1 us: add_block(): right_side = jnp.concatenate([partner[0], partner[1]], axis=1)]
    select_n x2 -> x0, other arithmetic: 8.18 us -> none  [shards(): return jnp.take(per_group, sched_row, axis=3)]
    gather x1 -> x0, local copies, waits for them, and re-layouts: 8.07 us -> none  [shards(): return jnp.take(per_group, sched_row, axis=3)]
  transfers between devices with their start and end apart: 1 -> 0, of which waited for: 1 -> 0; matrix products, arithmetic and copies ran while one was open for 2% -> 0% of each run, Pallas kernels for 0% -> 0%
where the time goes in v1:
time: 177 us; the launch traced here: 174 us
  Pallas kernels  155 us (88%)
  local copies, waits for them, and re-layouts  8.14 us (5%)
  other arithmetic  7.75 us (4%)
  matrix products  3.02 us (2%)
    pallas_call x1, Pallas kernels, cross(): pl.pallas_call(kernel, out_shape=jax.ShapeDtypeStruct((BINS, 2 * G * NGRP...  155 us
    unnamed x4, local copies, waits for them, and re-layouts  8.14 us
    convert_element_type x1, other arithmetic, shards(): white = (spectrum * weight[None, None, :, :]).astype(jnp.bfloat16)  3.58 us

profile of v1, /device:TPU:2, one launch (start us, length us, event | category | flops | bytes accessed | tf_op | source)
XLA Modules:
  0.0 174.0 jit_solution(10848237193160498201)
XLA Ops:
  0.0 0.8 copy.4
  0.8 1.2 cosine_convert_fusion
  2.1 2.9 %fusion = bf16[256,16,512]{2,1,0:T(8,128)(2,1)S(1)} fusion(bf16[256,16,512]{2,1,0:T(8,128)(2,1)} %param.3, s32[256,16]{1,0:T(8,128)S(1)} %copy.4), kind=kLoop, calls=%fused_computation.1 | loop fusion | flops 4194304 | bytes 8404992 | tf_op jit(solution)/shard_map/jit(_where)/select_n | solution.py:226
  5.0 0.0 copy-start
  5.0 3.0 %fusion.1 = (f32[16,256]{1,0:T(8,128)S(1)}, f32[256,16,256]{0,2,1:T(8,128)S(1)}) fusion(bf16[512,128]{0,1:T(8,128)(2,1)S(1)} %get-tuple-element.6, bf16[512,128]{0,1:T(8,128)(2,1)S(1)} %get-tuple-element.5, bf16[256,16,512]{2,1,0:T(8,128)(2,1)S(1)} %fusion), kind=kOutput, calls=%fused_computation.3 | convolution fusion | flops 1076359168 | bytes 8667136 | tf_op jit(solution)/shard_map/tk,ist->ksi/dot_general | solution.py:227
  8.0 0.0 copy-done
  8.1 3.6 %fusion.2 = bf16[2,128,16,256]{3,2,0,1:T(8,128)(2,1)} fusion(f32[2,128,16,256]{3,1,0,2:T(8,128)S(1)} %bitcast.19, f32[16,256]{1,0:T(8,128)S(1)} %rsqrt_select_fusion), kind=kLoop, calls=%fused_computation.5 | loop fusion | flops 2097152 | bytes 6307840 | tf_op jit(solution)/shard_map/convert_element_type | solution.py:232
  11.6 155.1 %shard_map.37 = bf16[4,4096,256]{2,1,0:T(8,128)(2,1)} custom-call(s32[8,8]{1,0:T(8,128)} %plan_ref.1, bf16[128,32,256]{2,1,0:T(8,128)(2,1)} %bitcast.18), custom_call_target="tpu_custom_call" | custom-call | tf_op jit(solution)/shard_map/pallas_call | solution.py:193
  166.7 7.3 %copy.15 = bf16[4,2,256,8,256]{4,3,2,1,0:T(8,128)(2,1)} copy(bf16[4,2,256,8,256]{4,3,2,1,0:T(8,128)(2,1)} %bitcast.17) | data formatting | bytes 16777216
  (2 shorter events, 0.0 us)
Async XLA Ops:
  5.0 3.0 %copy-start = (s32[256,16]{0,1:T(8,128)S(1)}, s32[256,16]{0,1:T(8,128)}, u32[]{:S(2)}) copy-start(s32[256,16]{0,1:T(8,128)} %param.4) | copy-start | bytes 49156

commit v2 on v1

v2 whole, which is shorter than its diff:
```python
import functools
import math

import jax
import jax.numpy as jnp
from jax import lax
from jax.experimental import pallas as pl
from jax.experimental.pallas import tpu as pltpu
from jax.sharding import PartitionSpec as P

F = 128
K0 = 2
MESH = pl.DeviceIdType.MESH

NY = 4
NZ = 2
NS = 32
PEERS = NZ * NS
BINS = 4
DEPTH = NS * 2 * 16
G = 256
NGRP = NZ * NY
TILE = 16
LAST = BINS - 1
AHEAD = 4
CUTS = [[(0, 0), (0, 128), (1, 0), (1, 128)]] * BINS


def make_basis(samples):
    times = jnp.arange(samples, dtype=jnp.int32)[:, None]
    bins = K0 + jnp.arange(F, dtype=jnp.int32)[None, :]
    phase = (times * bins % samples).astype(jnp.float32) * (2.0 * math.pi / samples)
    return jnp.concatenate([jnp.cos(phase), -jnp.sin(phase)], axis=1).astype(jnp.bfloat16)


def transpose_left(source, index, left):
    def step(c, carry):
        parts = source[index, pl.ds(c * 4, 4)]
        block = parts.reshape(128, G)
        turned = []
        for m in range(4):
            turned += [parts[m, 1], -parts[m, 0]]
        other = jnp.concatenate(turned, axis=0)
        at = pl.ds(pl.multiple_of(c * 128, 128), 128)
        left[pl.ds(0, G), at] = block.T
        left[pl.ds(G, G), at] = other.T
        return carry

    lax.fori_loop(0, DEPTH // 128, step, 0)


def product(left, right, index):
    full = jnp.dot(left[...], right[index].reshape(DEPTH, G), preferred_element_type=jnp.float32)
    return (full * (1.0 / 512.0)).astype(jnp.bfloat16)


def interleave(plan_ref, g, source, target, tmp, m):
    rows = pl.ds(pl.multiple_of(m * TILE, TILE), TILE)
    for r in range(NGRP):
        piece = source[plan_ref[g, r], rows, :].astype(jnp.float32)
        for h in range(2):
            tmp[h, pl.ds(r, TILE, NGRP), :] = piece[:, h * 128 : h * 128 + 128]
    at = pl.ds(pl.multiple_of(m * TILE * NGRP, TILE * NGRP), TILE * NGRP)
    for h in range(2):
        target[at, h * 128 : h * 128 + 128] = tmp[h].astype(jnp.bfloat16)


def kernel(plan_ref, white, mid, last, *scratch):
    spec = scratch[0:BINS]
    res = scratch[BINS : 2 * BINS - 1] + (last,)
    give, left, tmp = scratch[2 * BINS - 1 : 2 * BINS + 2]
    send1, recv1, send2, recv2, send3, recv3 = scratch[2 * BINS + 2 :]
    g = lax.axis_index("grp")
    s = lax.axis_index("seg")
    zh, y = lax.div(g, NY), lax.rem(g, NY)
    me = zh * NS + s
    right = zh * NY + lax.rem(y + 1, NY)
    leftd = zh * NY + lax.rem(y + NY - 1, NY)

    def peer(d):
        p = lax.rem(me + d, PEERS)
        return lax.div(p, NS), lax.rem(p, NS)

    barrier = pltpu.get_barrier_semaphore()

    def greet(d, carry):
        pz, ps = peer(d)
        pl.semaphore_signal(barrier, inc=1, device_id=(pz * NY + y, ps), device_id_type=MESH)
        return carry

    lax.fori_loop(1, PEERS, greet, 0)
    for n in (right, leftd):
        pl.semaphore_signal(barrier, inc=1, device_id=(n, s), device_id_type=MESH)
    pl.semaphore_wait(barrier, PEERS + 1)

    def cut(ref, where):
        part, lane = where
        lead = (slice(None),) * (len(ref.shape) - 3)
        if lane is None:
            return ref.at[lead + (part,)]
        return ref.at[lead + (part, slice(None), pl.ds(lane, 128))]

    def scatter(b, q):
        where = CUTS[b][q]

        def send(d, carry):
            pz, ps = peer(d)
            pltpu.make_async_remote_copy(
                src_ref=cut(white.at[ps * BINS + b], where),
                dst_ref=cut(spec[b].at[2 + zh, s], where),
                send_sem=send1.at[b, q],
                recv_sem=recv1.at[b, q],
                device_id=(pz * NY + y, ps),
                device_id_type=MESH,
            ).start()
            return carry

        lax.fori_loop(1, PEERS, send, 0)
        pltpu.make_async_copy(
            cut(white.at[s * BINS + b], where), cut(spec[b].at[2 + zh, s], where), recv1.at[b, q]
        ).start()

    def scatter_arrived(b, q):
        own = cut(spec[b].at[pl.ds(2, 2)], CUTS[b][q])
        pltpu.make_async_copy(own, own, recv1.at[b, q]).wait()

    def scatter_left(b, q):
        some = cut(white.at[pl.ds(0, PEERS - 1)], CUTS[b][q])
        pltpu.make_async_copy(some, some, send1.at[b, q]).wait()

    def neighbour(b, q, side):
        to, at = ((right, 0), (leftd, 4))[side]
        return pltpu.make_async_remote_copy(
            src_ref=cut(spec[b].at[pl.ds(2, 2)], CUTS[b][q]),
            dst_ref=cut(spec[b].at[pl.ds(at, 2)], CUTS[b][q]),
            send_sem=send2.at[b, q, side],
            recv_sem=recv2.at[b, q, side],
            device_id=(to, s),
            device_id_type=MESH,
        )

    def gift(b, side):
        to, group = ((right, lax.rem(y + 3, NY)), (leftd, NY + lax.rem(y + 1, NY)))[side]
        return pltpu.make_async_remote_copy(
            src_ref=give.at[b, side],
            dst_ref=res[b].at[group],
            send_sem=send3.at[b, side],
            recv_sem=recv3.at[b, side],
            device_id=(to, s),
            device_id_type=MESH,
        )

    def multiply(b):
        transpose_left(spec[b], 4 + zh, left)
        give[b, 0] = product(left, spec[b], 0)
        gift(b, 0).start()
        transpose_left(spec[b], zh, left)
        give[b, 1] = product(left, spec[b], 5)
        gift(b, 1).start()
        transpose_left(spec[b], 2 + zh, left)

        def block(t, carry):
            group = lax.rem(t, 2) * NY + lax.rem(y + 3 + lax.div(t, 2), NY)
            res[b][group] = product(left, spec[b], t)
            return carry

        lax.fori_loop(0, 6, block, 0)

    def assemble(b):
        def tile(m, carry):
            interleave(plan_ref, g, res[b], mid.at[b], tmp, m)
            return carry

        lax.fori_loop(0, 2 * G // TILE, tile, 0)

    def finish(b):
        for q in range(len(CUTS[b])):
            for side in range(2):
                neighbour(b, q, side).wait_recv()
        multiply(b)
        if b >= 1:
            for side in range(2):
                gift(b - 1, side).wait_recv()
            assemble(b - 1)

    steps = [(b, q) for b in range(BINS) for q in range(len(CUTS[b]))]
    ahead = AHEAD
    for b, q in steps[:ahead]:
        scatter(b, q)
    for k, (b, q) in enumerate(steps):
        scatter_arrived(b, q)
        for side in range(2):
            neighbour(b, q, side).start()
        while ahead < len(steps) and ahead <= k + AHEAD:
            scatter(*steps[ahead])
            ahead += 1
        if b >= 1 and q == 0:
            finish(b - 1)
    finish(LAST)
    for side in range(2):
        gift(LAST, side).wait_recv()
    for b, q in steps:
        scatter_left(b, q)
        for side in range(2):
            neighbour(b, q, side).wait_send()
    for b in range(BINS):
        for side in range(2):
            gift(b, side).wait_send()


def cross(plan, white):
    bf16 = jnp.bfloat16
    most = max(len(c) for c in CUTS)
    return pl.pallas_call(
        kernel,
        out_shape=(
            pltpu.VMEM((LAST, 2 * G * NGRP, G), bf16),
            pltpu.VMEM((NGRP, 2 * G, G), bf16),
        ),
        in_specs=[
            pl.BlockSpec(memory_space=pltpu.SMEM),
            pl.BlockSpec(memory_space=pltpu.VMEM),
        ],
        out_specs=(pl.BlockSpec(memory_space=pltpu.VMEM),) * 2,
        scratch_shapes=[pltpu.VMEM((6, NS, 2, TILE, G), bf16)] * BINS
        + [pltpu.VMEM((NGRP, 2 * G, G), bf16)] * LAST
        + [
            pltpu.VMEM((BINS, 2, 2 * G, G), bf16),
            pltpu.VMEM((2 * G, DEPTH), bf16),
            pltpu.VMEM((2, TILE * NGRP, 128), jnp.float32),
            pltpu.SemaphoreType.DMA((BINS, most)),
            pltpu.SemaphoreType.DMA((BINS, most)),
            pltpu.SemaphoreType.DMA((BINS, most, 2)),
            pltpu.SemaphoreType.DMA((BINS, most, 2)),
            pltpu.SemaphoreType.DMA((BINS, 2)),
            pltpu.SemaphoreType.DMA((BINS, 2)),
        ],
        compiler_params=pltpu.CompilerParams(
            collective_id=0, has_side_effects=True, vmem_limit_bytes=36 * 1024 * 1024
        ),
    )(plan, pltpu.with_memory_space_constraint(white, pltpu.VMEM))


QUARTERS = 4


def place_kernel(plan_ref, mid, last, out, target, tmp, mid_sem, out_sem):
    g = lax.axis_index("grp")

    def keep(b):
        return pltpu.make_async_copy(mid.at[b], out.at[b], mid_sem.at[b])

    for b in range(LAST):
        keep(b).start()
    size = 2 * G * NGRP // QUARTERS

    def store(q):
        rows = pl.ds(q * size, size)
        return pltpu.make_async_copy(target.at[rows], out.at[LAST, rows], out_sem.at[q])

    def tile(m, carry):
        interleave(plan_ref, g, last, target, tmp, m)
        return carry

    each = 2 * G // TILE // QUARTERS
    for q in range(QUARTERS):
        lax.fori_loop(q * each, (q + 1) * each, tile, 0)
        store(q).start()
    for q in range(QUARTERS):
        store(q).wait()
    for b in range(LAST):
        keep(b).wait()


def place(plan, mid, last):
    bf16 = jnp.bfloat16
    return pl.pallas_call(
        place_kernel,
        out_shape=jax.ShapeDtypeStruct((BINS, 2 * G * NGRP, G), bf16),
        in_specs=[
            pl.BlockSpec(memory_space=pltpu.SMEM),
            pl.BlockSpec(memory_space=pltpu.VMEM),
            pl.BlockSpec(memory_space=pltpu.VMEM),
        ],
        out_specs=pl.BlockSpec(memory_space=pl.ANY),
        scratch_shapes=[
            pltpu.VMEM((2 * G * NGRP, G), bf16),
            pltpu.VMEM((2, TILE * NGRP, 128), jnp.float32),
            pltpu.SemaphoreType.DMA((LAST,)),
            pltpu.SemaphoreType.DMA((QUARTERS,)),
        ],
        compiler_params=pltpu.CompilerParams(vmem_limit_bytes=16 * 1024 * 1024),
    )(
        plan,
        pltpu.with_memory_space_constraint(mid, pltpu.VMEM),
        pltpu.with_memory_space_constraint(last, pltpu.VMEM),
    )


def shards(waveform, valid_count, plan):
    group_rows, seg_local, samples = waveform.shape
    basis = make_basis(samples)
    times = lax.broadcasted_iota(jnp.int32, waveform.shape, 2)
    gated = jnp.where(times < valid_count[:, :, None], waveform, jnp.zeros_like(waveform))
    spectrum = jnp.einsum("tk,ist->ksi", basis, gated, preferred_element_type=jnp.float32)
    spectrum = spectrum.reshape(2, F, seg_local, group_rows)
    power = jnp.sum(spectrum * spectrum, axis=(0, 1)) / F
    keep = (valid_count.T >= samples // 2).astype(jnp.float32)
    weight = keep / jnp.sqrt(power + 1e-06)
    white = (spectrum * weight[None, None, :, :]).astype(jnp.bfloat16)
    white = white.transpose(1, 0, 2, 3)
    mid, last = cross(plan, white)
    return place(plan, mid, last).reshape(BINS, 2, G, NGRP, G)


def solution(mesh):
    return jax.shard_map(
        shards,
        mesh=mesh,
        in_specs=(P("grp", "seg", None), P("grp", "seg"), P()),
        out_specs=P("seg", None, "grp", None, None),
        check_vma=False,
    )
```

time: 177 us -> 155 us (0.88); the launches traced: 174 us -> 154 us
  Pallas kernels: 155 us -> 144 us
  local copies, waits for them, and re-layouts: 8.14 us -> 0.83 us
    pallas_call x1 -> x2, Pallas kernels: 155 us -> 144 us  [the longest x1 140 us: cross(): pl.pallas_call(kernel, out_shape=(pltpu.VMEM((LAST, 2 * G * NGRP, G), bf1...]
    unnamed x4 -> x5, local copies, waits for them, and re-layouts: 8.14 us -> 0.83 us
    convert_element_type x1 -> x0, other arithmetic: 3.58 us -> none  [shards(): white = (spectrum * weight[None, None, :, :]).astype(jnp.bfloat16)]
    transpose x0 -> x1, other arithmetic: none -> 2.26 us  [shards(): white = white.transpose(1, 0, 2, 3)]
where the time goes in v2:
time: 155 us; the launch traced here: 154 us
  Pallas kernels  144 us (93%)
  other arithmetic  6.43 us (4%)
  matrix products  3.02 us (2%)
    pallas_call x1, Pallas kernels, cross(): pl.pallas_call(kernel, out_shape=(pltpu.VMEM((LAST, 2 * G * NGRP, G), bf1...  140 us
    pallas_call x1, Pallas kernels, place(): pl.pallas_call(place_kernel, out_shape=jax.ShapeDtypeStruct((BINS, 2 * G...  3.94 us

profile of v2, /device:TPU:2, one launch (start us, length us, event | category | flops | bytes accessed | tf_op | source)
XLA Modules:
  0.0 154.0 jit_solution(17115272908361555421)
XLA Ops:
  0.0 0.8 copy.6
  0.8 1.2 cosine_convert_fusion
  2.1 2.9 %fusion = bf16[256,16,512]{2,1,0:T(8,128)(2,1)S(1)} fusion(bf16[256,16,512]{2,1,0:T(8,128)(2,1)} %param.3, s32[256,16]{1,0:T(8,128)S(1)} %copy.6), kind=kLoop, calls=%fused_computation.1 | loop fusion | flops 4194304 | bytes 8404992 | tf_op jit(solution)/shard_map/jit(_where)/select_n | solution.py:304
  5.0 0.0 copy-start.1
  5.0 3.0 %fusion.2 = (f32[16,256]{1,0:T(8,128)S(1)}, f32[256,16,256]{0,2,1:T(8,128)S(1)}) fusion(bf16[512,128]{0,1:T(8,128)(2,1)S(1)} %get-tuple-element.10, bf16[512,128]{0,1:T(8,128)(2,1)S(1)} %get-tuple-element.9, bf16[256,16,512]{2,1,0:T(8,128)(2,1)S(1)} %fusion), kind=kOutput, calls=%fused_computation.5 | convolution fusion | flops 1076359168 | bytes 8667136 | tf_op jit(solution)/shard_map/tk,ist->ksi/dot_general | solution.py:305
  8.0 0.0 copy-start
  8.0 0.0 copy-done.1
  8.1 2.3 %fusion.5.white = bf16[128,2,16,256]{3,2,1,0:T(8,128)(2,1)S(1)} fusion(f32[2,128,16,256]{3,1,0,2:T(8,128)S(1)} %bitcast.16, f32[16,256]{1,0:T(8,128)S(1)} %rsqrt_select_fusion), kind=kLoop, calls=%fused_computation.8 | loop fusion | flops 2097152 | bytes 6307840 | tf_op jit(solution)/shard_map/transpose | solution.py:311
  10.3 0.0 copy-done
  10.4 139.7 %shard_map.37 = (bf16[3,4096,256]{2,1,0:T(8,128)(2,1)S(1)}, bf16[8,512,256]{2,1,0:T(8,128)(2,1)S(1)}) custom-call(s32[8,8]{1,0:T(8,128)S(1)} %copy-done, bf16[128,2,16,256]{3,2,1,0:T(8,128)(2,1)S(1)} %fusion.5.white), custom_call_target="tpu_custom_call" | custom-call | tf_op jit(solution)/shard_map/pallas_call | solution.py:214
  150.1 3.9 %shard_map.38 = bf16[4,4096,256]{2,1,0:T(8,128)(2,1)} custom-call(s32[8,8]{1,0:T(8,128)S(1)} %copy-done, bf16[3,4096,256]{2,1,0:T(8,128)(2,1)S(1)} %get-tuple-element.7.mid, bf16[8,512,256]{2,1,0:T(8,128)(2,1)S(1)} %get-tuple-element.8.last), custom_call_target="tpu_custom_call" | custom-call | tf_op jit(solution)/shard_map/pallas_call | solution.py:277
  (2 shorter events, 0.0 us)
Async XLA Ops:
  5.0 3.1 %copy-start.1 = (s32[256,16]{0,1:T(8,128)S(1)}, s32[256,16]{0,1:T(8,128)}, u32[]{:S(2)}) copy-start(s32[256,16]{0,1:T(8,128)} %param.4) | copy-start | bytes 49156
  8.0 2.3 %copy-start = (s32[8,8]{1,0:T(8,128)S(1)}, s32[8,8]{1,0:T(8,128)}, u32[]{:S(2)}) copy-start(s32[8,8]{1,0:T(8,128)} %plan_ref.3) | copy-start | bytes 772

commit v3 on v2

--- a/solution.py
+++ b/solution.py
@@ -3,6 +3,7 @@
 
 import jax
 import jax.numpy as jnp
+import numpy as np
 from jax import lax
 from jax.experimental import pallas as pl
 from jax.experimental.pallas import tpu as pltpu
@@ -27,10 +28,43 @@
 
 
 def make_basis(samples):
-    times = jnp.arange(samples, dtype=jnp.int32)[:, None]
-    bins = K0 + jnp.arange(F, dtype=jnp.int32)[None, :]
-    phase = (times * bins % samples).astype(jnp.float32) * (2.0 * math.pi / samples)
-    return jnp.concatenate([jnp.cos(phase), -jnp.sin(phase)], axis=1).astype(jnp.bfloat16)
+    times = np.arange(samples, dtype=np.int32)[:, None]
+    bins = K0 + np.arange(F, dtype=np.int32)[None, :]
+    phase = (times * bins % samples).astype(np.float32) * np.float32(2.0 * math.pi / samples)
+    return np.concatenate([np.cos(phase), -np.sin(phase)], axis=1).astype(jnp.bfloat16)
+
+
+CHUNKS = 2
+
+
+def whiten(wave, valid, basis, out, held, rows, turned, counts, sem):
+    size = G // CHUNKS
+
+    def load(c):
+        return pltpu.make_async_copy(wave.at[pl.ds(c * size, size)], held.at[c], sem.at[c])
+
+    for c in range(CHUNKS):
+        load(c).start()
+    samples = held.shape[-1]
+    count = valid[...].T
+    counts[...] = jnp.where(count >= samples // 2, count, 0)
+    for c in range(CHUNKS):
+        load(c).wait()
+        limit = counts[pl.ds(c * size, size), :]
+        times = lax.broadcasted_iota(jnp.int32, (size, TILE, samples), 2)
+        gated = jnp.where(times < limit[:, :, None], held[c].astype(jnp.float32), 0.0)
+        gated = gated.astype(jnp.bfloat16).reshape(size * TILE, samples)
+        spectrum = jnp.dot(gated, basis[...], preferred_element_type=jnp.float32)
+        power = jnp.sum(spectrum * spectrum, axis=1, keepdims=True) * (1.0 / F)
+        spectrum = spectrum * lax.rsqrt(power + 1e-06)
+        for h in range(2):
+            rows[h] = spectrum[:, h * 128 : h * 128 + 128]
+        for k in range(TILE):
+            for h in range(2):
+                turned[h, pl.ds(k, F, TILE), :] = rows[h, pl.ds(k, size, TILE), :].T
+        for h in range(2):
+            block = turned[h].reshape(F, TILE, size).astype(jnp.bfloat16)
+            out[:, h, :, c * size : c * size + size] = block
 
 
 def transpose_left(source, index, left):
@@ -65,11 +99,12 @@
         target[at, h * 128 : h * 128 + 128] = tmp[h].astype(jnp.bfloat16)
 
 
-def kernel(plan_ref, white, mid, last, *scratch):
+def kernel(plan_ref, wave, valid, basis, mid, last, *scratch):
     spec = scratch[0:BINS]
     res = scratch[BINS : 2 * BINS - 1] + (last,)
     give, left, tmp = scratch[2 * BINS - 1 : 2 * BINS + 2]
-    send1, recv1, send2, recv2, send3, recv3 = scratch[2 * BINS + 2 :]
+    send1, recv1, send2, recv2, send3, recv3 = scratch[2 * BINS + 2 : -6]
+    white = scratch[-6]
     g = lax.axis_index("grp")
     s = lax.axis_index("seg")
     zh, y = lax.div(g, NY), lax.rem(g, NY)
@@ -88,9 +123,10 @@
         pl.semaphore_signal(barrier, inc=1, device_id=(pz * NY + y, ps), device_id_type=MESH)
         return carry
 
-    lax.fori_loop(1, PEERS, greet, 0)
+    lax.fori_loop(1, PEERS, greet, 0, unroll=7)
     for n in (right, leftd):
         pl.semaphore_signal(barrier, inc=1, device_id=(n, s), device_id_type=MESH)
+    whiten(wave, valid, basis, *scratch[-6:])
     pl.semaphore_wait(barrier, PEERS + 1)
 
     def cut(ref, where):
@@ -115,7 +151,7 @@
             ).start()
             return carry
 
-        lax.fori_loop(1, PEERS, send, 0)
+        lax.fori_loop(1, PEERS, send, 0, unroll=7)
         pltpu.make_async_copy(
             cut(white.at[s * BINS + b], where), cut(spec[b].at[2 + zh, s], where), recv1.at[b, q]
         ).start()
@@ -208,8 +244,9 @@
             gift(b, side).wait_send()
 
 
-def cross(plan, white):
+def cross(plan, waveform, valid_count):
     bf16 = jnp.bfloat16
+    samples = waveform.shape[-1]
     most = max(len(c) for c in CUTS)
     return pl.pallas_call(
         kernel,
@@ -219,6 +256,8 @@
         ),
         in_specs=[
             pl.BlockSpec(memory_space=pltpu.SMEM),
+            pl.BlockSpec(memory_space=pl.ANY),
+            pl.BlockSpec(memory_space=pltpu.VMEM),
             pl.BlockSpec(memory_space=pltpu.VMEM),
         ],
         out_specs=(pl.BlockSpec(memory_space=pltpu.VMEM),) * 2,
@@ -234,11 +273,17 @@
             pltpu.SemaphoreType.DMA((BINS, most, 2)),
             pltpu.SemaphoreType.DMA((BINS, 2)),
             pltpu.SemaphoreType.DMA((BINS, 2)),
+            pltpu.VMEM((F, 2, TILE, G), bf16),
+            pltpu.VMEM((CHUNKS, G // CHUNKS, TILE, samples), bf16),
+            pltpu.VMEM((2, G // CHUNKS * TILE, 128), jnp.float32),
+            pltpu.VMEM((2, F * TILE, G // CHUNKS), jnp.float32),
+            pltpu.VMEM((G, TILE), jnp.int32),
+            pltpu.SemaphoreType.DMA((CHUNKS,)),
         ],
         compiler_params=pltpu.CompilerParams(
-            collective_id=0, has_side_effects=True, vmem_limit_bytes=36 * 1024 * 1024
+            collective_id=0, has_side_effects=True, vmem_limit_bytes=52 * 1024 * 1024
         ),
-    )(plan, pltpu.with_memory_space_constraint(white, pltpu.VMEM))
+    )(plan, waveform, valid_count.T, make_basis(samples))
 
 
 QUARTERS = 4
@@ -298,18 +343,7 @@
 
 
 def shards(waveform, valid_count, plan):
-    group_rows, seg_local, samples = waveform.shape
-    basis = make_basis(samples)
-    times = lax.broadcasted_iota(jnp.int32, waveform.shape, 2)
-    gated = jnp.where(times < valid_count[:, :, None], waveform, jnp.zeros_like(waveform))
-    spectrum = jnp.einsum("tk,ist->ksi", basis, gated, preferred_element_type=jnp.float32)
-    spectrum = spectrum.reshape(2, F, seg_local, group_rows)
-    power = jnp.sum(spectrum * spectrum, axis=(0, 1)) / F
-    keep = (valid_count.T >= samples // 2).astype(jnp.float32)
-    weight = keep / jnp.sqrt(power + 1e-06)
-    white = (spectrum * weight[None, None, :, :]).astype(jnp.bfloat16)
-    white = white.transpose(1, 0, 2, 3)
-    mid, last = cross(plan, white)
+    mid, last = cross(plan, waveform, valid_count)
     return place(plan, mid, last).reshape(BINS, 2, G, NGRP, G)
 
 

time: 155 us -> 150 us (0.968)
  other arithmetic: 6.43 us -> 0 us
  Pallas kernels: 144 us -> 148 us
  matrix products: 3.02 us -> 0 us
    pallas_call x1, Pallas kernels: 140 us -> 144 us  [cross(): pl.pallas_call(kernel, out_shape=(pltpu.VMEM((LAST, 2 * G * NGRP, G), bf1...]
    dot_general x1 -> x0, matrix products: 3.02 us -> none  [shards(): jnp.einsum('tk,ist->ksi', basis, gated, preferred_element_type=jnp.float32)]
    select_n x1 -> x0, other arithmetic: 2.91 us -> none  [shards(): jnp.where(times < valid_count[:, :, None], waveform, jnp.zeros_like(wavef...]
    transpose x1 -> x0, other arithmetic: 2.26 us -> none  [shards(): white = white.transpose(1, 0, 2, 3)]
where the time goes in v3:
time: 150 us; the launch traced here: 149 us
  Pallas kernels  148 us (99%)
    pallas_call x1, Pallas kernels, cross(): pl.pallas_call(kernel, out_shape=(pltpu.VMEM((LAST, 2 * G * NGRP, G), bf1...  144 us
    pallas_call x1, Pallas kernels, place(): pl.pallas_call(place_kernel, out_shape=jax.ShapeDtypeStruct((BINS, 2 * G...  3.94 us

profile of v3, /device:TPU:2, one launch (start us, length us, event | category | flops | bytes accessed | tf_op | source)
XLA Modules:
  0.0 149.0 jit_solution(10235812108040833681)
XLA Ops:
  0.0 144.4 %shard_map.46 = (bf16[3,4096,256]{2,1,0:T(8,128)(2,1)S(1)}, bf16[8,512,256]{2,1,0:T(8,128)(2,1)S(1)}) custom-call(s32[8,8]{1,0:T(8,128)} %plan_ref.3, bf16[256,16,512]{2,1,0:T(8,128)(2,1)} %wave.1, s32[16,256]{1,0:T(8,128)} %bitcast.2, bf16[512,256]{1,0:T(8,128)(2,1)} %constant.2.clone.basis), custom_call_target="tpu_custom_call" | custom-call | tf_op jit(solution)/shard_map/pallas_call | solution.py:251
  144.4 0.0 copy-start
  144.4 0.7 copy-done
  145.1 3.9 %shard_map.47 = bf16[4,4096,256]{2,1,0:T(8,128)(2,1)} custom-call(s32[8,8]{1,0:T(8,128)S(1)} %copy-done, bf16[3,4096,256]{2,1,0:T(8,128)(2,1)S(1)} %get-tuple-element.7.mid, bf16[8,512,256]{2,1,0:T(8,128)(2,1)S(1)} %get-tuple-element.8.last), custom_call_target="tpu_custom_call" | custom-call | tf_op jit(solution)/shard_map/pallas_call | solution.py:322
Async XLA Ops:
  144.4 0.7 copy-start

commit v4 on v3

--- a/solution.py
+++ b/solution.py
@@ -37,28 +37,38 @@
 CHUNKS = 2
 
 
+PIECE = 128
+
+
+def load_wave(wave, held, sem, n):
+    some = pl.ds(pl.multiple_of(n * PIECE, PIECE), PIECE)
+    return pltpu.make_async_copy(wave.at[some], held.at[some], sem.at[n])
+
+
 def whiten(wave, valid, basis, out, held, rows, turned, counts, sem):
     size = G // CHUNKS
-
-    def load(c):
-        return pltpu.make_async_copy(wave.at[pl.ds(c * size, size)], held.at[c], sem.at[c])
-
-    for c in range(CHUNKS):
-        load(c).start()
     samples = held.shape[-1]
     count = valid[...].T
     counts[...] = jnp.where(count >= samples // 2, count, 0)
+
     for c in range(CHUNKS):
-        load(c).wait()
-        limit = counts[pl.ds(c * size, size), :]
-        times = lax.broadcasted_iota(jnp.int32, (size, TILE, samples), 2)
-        gated = jnp.where(times < limit[:, :, None], held[c].astype(jnp.float32), 0.0)
-        gated = gated.astype(jnp.bfloat16).reshape(size * TILE, samples)
-        spectrum = jnp.dot(gated, basis[...], preferred_element_type=jnp.float32)
-        power = jnp.sum(spectrum * spectrum, axis=1, keepdims=True) * (1.0 / F)
-        spectrum = spectrum * lax.rsqrt(power + 1e-06)
-        for h in range(2):
-            rows[h] = spectrum[:, h * 128 : h * 128 + 128]
+        def piece(m, carry):
+            n = c * (size // PIECE) + m
+            load_wave(wave, held, sem, n).wait()
+            some = pl.ds(pl.multiple_of(n * PIECE, PIECE), PIECE)
+            limit = counts[some, :]
+            times = lax.broadcasted_iota(jnp.int32, (PIECE, TILE, samples), 2)
+            gated = jnp.where(times < limit[:, :, None], held[some].astype(jnp.float32), 0.0)
+            gated = gated.astype(jnp.bfloat16).reshape(PIECE * TILE, samples)
+            spectrum = jnp.dot(gated, basis[...], preferred_element_type=jnp.float32)
+            power = jnp.sum(spectrum * spectrum, axis=1, keepdims=True) * (1.0 / F)
+            spectrum = spectrum * lax.rsqrt(power + 1e-06)
+            at = pl.ds(pl.multiple_of(m * PIECE * TILE, PIECE * TILE), PIECE * TILE)
+            for h in range(2):
+                rows[h, at, :] = spectrum[:, h * 128 : h * 128 + 128]
+            return carry
+
+        lax.fori_loop(0, size // PIECE, piece, 0)
         for k in range(TILE):
             for h in range(2):
                 turned[h, pl.ds(k, F, TILE), :] = rows[h, pl.ds(k, size, TILE), :].T
@@ -104,7 +114,10 @@
     res = scratch[BINS : 2 * BINS - 1] + (last,)
     give, left, tmp = scratch[2 * BINS - 1 : 2 * BINS + 2]
     send1, recv1, send2, recv2, send3, recv3 = scratch[2 * BINS + 2 : -6]
-    white = scratch[-6]
+    white, held = scratch[-6], scratch[-5]
+    wave_sem = scratch[-1]
+    for n in range(G // PIECE):
+        load_wave(wave, held, wave_sem, n).start()
     g = lax.axis_index("grp")
     s = lax.axis_index("seg")
     zh, y = lax.div(g, NY), lax.rem(g, NY)
@@ -274,11 +287,11 @@
             pltpu.SemaphoreType.DMA((BINS, 2)),
             pltpu.SemaphoreType.DMA((BINS, 2)),
             pltpu.VMEM((F, 2, TILE, G), bf16),
-            pltpu.VMEM((CHUNKS, G // CHUNKS, TILE, samples), bf16),
+            pltpu.VMEM((G, TILE, samples), bf16),
             pltpu.VMEM((2, G // CHUNKS * TILE, 128), jnp.float32),
             pltpu.VMEM((2, F * TILE, G // CHUNKS), jnp.float32),
             pltpu.VMEM((G, TILE), jnp.int32),
-            pltpu.SemaphoreType.DMA((CHUNKS,)),
+            pltpu.SemaphoreType.DMA((G // PIECE,)),
         ],
         compiler_params=pltpu.CompilerParams(
             collective_id=0, has_side_effects=True, vmem_limit_bytes=52 * 1024 * 1024
@@ -289,14 +302,17 @@
 QUARTERS = 4
 
 
-def place_kernel(plan_ref, mid, last, out, target, tmp, mid_sem, out_sem):
+def place_kernel(plan, mid, last, out, plan_ref, target, tmp, plan_sem, mid_sem, out_sem):
     g = lax.axis_index("grp")
 
     def keep(b):
         return pltpu.make_async_copy(mid.at[b], out.at[b], mid_sem.at[b])
 
+    fetch = pltpu.make_async_copy(plan, plan_ref, plan_sem)
+    fetch.start()
     for b in range(LAST):
         keep(b).start()
+    fetch.wait()
     size = 2 * G * NGRP // QUARTERS
 
     def store(q):
@@ -323,20 +339,22 @@
         place_kernel,
         out_shape=jax.ShapeDtypeStruct((BINS, 2 * G * NGRP, G), bf16),
         in_specs=[
-            pl.BlockSpec(memory_space=pltpu.SMEM),
+            pl.BlockSpec(memory_space=pltpu.HBM),
             pl.BlockSpec(memory_space=pltpu.VMEM),
             pl.BlockSpec(memory_space=pltpu.VMEM),
         ],
         out_specs=pl.BlockSpec(memory_space=pl.ANY),
         scratch_shapes=[
+            pltpu.SMEM((NGRP, plan.shape[1]), jnp.int32),
             pltpu.VMEM((2 * G * NGRP, G), bf16),
             pltpu.VMEM((2, TILE * NGRP, 128), jnp.float32),
+            pltpu.SemaphoreType.DMA,
             pltpu.SemaphoreType.DMA((LAST,)),
             pltpu.SemaphoreType.DMA((QUARTERS,)),
         ],
         compiler_params=pltpu.CompilerParams(vmem_limit_bytes=16 * 1024 * 1024),
     )(
-        plan,
+        pltpu.with_memory_space_constraint(plan, pltpu.HBM),
         pltpu.with_memory_space_constraint(mid, pltpu.VMEM),
         pltpu.with_memory_space_constraint(last, pltpu.VMEM),
     )

time: 150 us -> 148 us (0.987)
  no operation moved by 1% of the time
where the time goes in v4:
time: 148 us; the launch traced here: 147 us
  Pallas kernels  147 us (99%)
    pallas_call x1, Pallas kernels, cross(): pl.pallas_call(kernel, out_shape=(pltpu.VMEM((LAST, 2 * G * NGRP, G), bf1...  143 us
    pallas_call x1, Pallas kernels, place(): pl.pallas_call(place_kernel, out_shape=jax.ShapeDtypeStruct((BINS, 2 * G...  3.35 us

profile of v4, /device:TPU:2, one launch (start us, length us, event | category | flops | bytes accessed | tf_op | source)
XLA Modules:
  0.0 146.6 jit_solution(14964413611316629412)
XLA Ops:
  0.0 143.2 %shard_map.46 = (bf16[3,4096,256]{2,1,0:T(8,128)(2,1)S(1)}, bf16[8,512,256]{2,1,0:T(8,128)(2,1)S(1)}) custom-call(s32[8,8]{1,0:T(8,128)} %plan.1, bf16[256,16,512]{2,1,0:T(8,128)(2,1)} %wave.1, s32[16,256]{1,0:T(8,128)} %bitcast.2, bf16[512,256]{1,0:T(8,128)(2,1)} %constant.2.clone.basis), custom_call_target="tpu_custom_call" | custom-call | tf_op jit(solution)/shard_map/pallas_call | solution.py:264
  143.2 3.4 %shard_map.47 = bf16[4,4096,256]{2,1,0:T(8,128)(2,1)} custom-call(s32[8,8]{1,0:T(8,128)} %plan.1, bf16[3,4096,256]{2,1,0:T(8,128)(2,1)S(1)} %get-tuple-element.7.mid, bf16[8,512,256]{2,1,0:T(8,128)(2,1)S(1)} %get-tuple-element.8.last), custom_call_target="tpu_custom_call" | custom-call | tf_op jit(solution)/shard_map/pallas_call | solution.py:338

commit v5 on v4

--- a/solution.py
+++ b/solution.py
@@ -90,7 +90,7 @@
         left[pl.ds(G, G), at] = other.T
         return carry
 
-    lax.fori_loop(0, DEPTH // 128, step, 0)
+    lax.fori_loop(0, DEPTH // 128, step, 0, unroll=4)
 
 
 def product(left, right, index):

time: 148 us -> 147 us (level)
  no operation moved by 1% of the time
where the time goes in v5:
time: 147 us; the launch traced here: 146 us
  Pallas kernels  146 us (99%)
    pallas_call x1, Pallas kernels, cross(): pl.pallas_call(kernel, out_shape=(pltpu.VMEM((LAST, 2 * G * NGRP, G), bf1...  143 us
    pallas_call x1, Pallas kernels, place(): pl.pallas_call(place_kernel, out_shape=jax.ShapeDtypeStruct((BINS, 2 * G...  3.35 us

profile of v5, /device:TPU:2, one launch (start us, length us, event | category | flops | bytes accessed | tf_op | source)
XLA Modules:
  0.0 146.3 jit_solution(10883844376047428065)
XLA Ops:
  0.0 143.0 %shard_map.46 = (bf16[3,4096,256]{2,1,0:T(8,128)(2,1)S(1)}, bf16[8,512,256]{2,1,0:T(8,128)(2,1)S(1)}) custom-call(s32[8,8]{1,0:T(8,128)} %plan.1, bf16[256,16,512]{2,1,0:T(8,128)(2,1)} %wave.1, s32[16,256]{1,0:T(8,128)} %bitcast.2, bf16[512,256]{1,0:T(8,128)(2,1)} %constant.2.clone.basis), custom_call_target="tpu_custom_call" | custom-call | tf_op jit(solution)/shard_map/pallas_call | solution.py:264
  143.0 3.4 %shard_map.47 = bf16[4,4096,256]{2,1,0:T(8,128)(2,1)} custom-call(s32[8,8]{1,0:T(8,128)} %plan.1, bf16[3,4096,256]{2,1,0:T(8,128)(2,1)S(1)} %get-tuple-element.7.mid, bf16[8,512,256]{2,1,0:T(8,128)(2,1)S(1)} %get-tuple-element.8.last), custom_call_target="tpu_custom_call" | custom-call | tf_op jit(solution)/shard_map/pallas_call | solution.py:338
